TPU v7x, 512 devices: a whole 4x8x8 slice. The times are simulated.
512 devices in a mesh: pool: 4 (over y_hi, core), grp: 32 (over z, x), tp: 4 (over y_lo).
Axes of the slice: x: 4, y: 8 (y_hi: 2, y_lo: 4; y = y_hi * 4 + y_lo), z: 8, core: 2. Of those that a mesh axis runs over, the one named last changes fastest.
Arguments:
- history: bfloat16 [32768, 3584], P(('grp', 'tp')), may hold values from -60 to 60
- norm_gain: float32 [3584], replicated, may hold values from 0.5 to 2
- key_value_weight: bfloat16 [3584, 1024], P('tp', 'pool'), may hold values from -0.09375 to 0.09375
- query_weight: bfloat16 [3584, 3584], P('tp', 'pool'), may hold values from -0.09375 to 0.09375
- live_count: int32 [4096], P(('grp', 'tp')), may hold values from 1 to 8
- owner_group: int32 [4096, 1], P(('grp', 'tp')), may hold values from 0 to 31; in each aligned block of 32 rows (0 to 31, 32 to 63, ...) at most 2 rows name the same one
- code_table: bfloat16 [512, 3584], P('pool', 'tp'), may hold values from -60 to 60
- code_ids: int32 [4, 4096], P(None, 'grp'), may hold values from 0 to 511
- key_value_cache: bfloat16 [4096, 16, 1024], P(('grp', 'tp'), None, 'pool'), may hold values from -700 to 700
Outputs:
- attended: bfloat16 [4, 4096, 3584], P(None, ('grp', 'tp'), 'pool')
- fresh_blocks: bfloat16 [32, 4, 32, 2, 8, 1024], P('grp', 'tp', None, None, None, 'pool')
Inputs may be any that keep to these rules, and one draw needn't show every extreme that they name: `owner_group`: among the 32 blocks of one device no owner group is named more than 2 times, and some device names some group exactly 2 times.
All inputs are finite; a program needn't handle non-finite values.
Results may differ from a plain program's by a relative error of at most 0.02705.
Values may be sent and summed in bfloat16 or wider, within the bound.
No kernel may reach another device: no remote copies, remote signals or barrier semaphores. Data moves between devices by JAX's collectives and lax.ppermute only.
A program may use at most 64 MiB of HBM per device.

v0:
```python
import math

import jax
import jax.numpy as jnp
from jax import lax
from jax.sharding import PartitionSpec as P

MODEL_WIDTH = 3584
HEAD_SIZE = 128


EPSILON = 1e-06


def shards(
    history,
    norm_gain,
    key_value_weight,
    query_weight,
    live_count,
    owner_group,
    code_table,
    code_ids,
    key_value_cache,
):
    hist_f32 = history.astype(jnp.float32)
    hist_scale = lax.rsqrt(jnp.mean(hist_f32 * hist_f32, axis=-1, keepdims=True) + EPSILON)
    hist_normed = (hist_f32 * norm_gain).astype(jnp.bfloat16)
    kv_sum = jnp.dot(
        hist_normed,
        lax.all_gather(key_value_weight, "tp", axis=0, tiled=True),
        preferred_element_type=jnp.float32,
    )
    hist_kv = (hist_scale * kv_sum).astype(jnp.bfloat16)
    blocks_here = live_count.shape[0]
    block_len = history.shape[0] // blocks_here
    key_value_width = key_value_weight.shape[1]
    groups = lax.axis_size("grp")
    capacity = max(2, 2 * blocks_here // groups)
    events = lax.broadcasted_iota(jnp.int32, (blocks_here, block_len), 1)
    keep = events < live_count[:, None]
    blocks = jnp.where(
        keep[:, :, None],
        hist_kv.reshape(blocks_here, block_len, key_value_width),
        jnp.zeros((), jnp.bfloat16),
    )
    target = owner_group[:, 0]
    same_target = target[:, None] == target[None, :]
    order = lax.iota(jnp.int32, blocks_here)
    earlier = order[None, :] < order[:, None]
    rank = jnp.sum((same_target & earlier).astype(jnp.int32), axis=1)
    group_ids = lax.iota(jnp.int32, groups)
    slot_ids = lax.iota(jnp.int32, capacity)
    select = (
        (target[None, None, :] == group_ids[:, None, None])
        & (rank[None, None, :] == slot_ids[None, :, None])
    ).astype(jnp.bfloat16)
    outgoing = jnp.einsum(
        "gkb,bx->gkx",
        select,
        blocks.reshape(blocks_here, block_len * key_value_width),
        preferred_element_type=jnp.float32,
    )
    outgoing = outgoing.astype(jnp.bfloat16).reshape(groups, capacity, block_len, key_value_width)
    received = lax.all_to_all(outgoing, "grp", split_axis=0, concat_axis=0, tiled=True)
    fresh_blocks = received[None, None]
    steps, group_rows = code_ids.shape
    flat_ids = code_ids.reshape(-1)
    local_codes = code_table.shape[0]
    first_code = lax.axis_index("pool") * local_codes
    codes = first_code + lax.iota(jnp.int32, local_codes)
    one_hot = (flat_ids[:, None] == codes[None, :]).astype(jnp.bfloat16)
    partial_rows = jnp.dot(one_hot, code_table, preferred_element_type=jnp.float32)
    tokens = lax.psum(partial_rows.astype(jnp.bfloat16), "pool")
    quarter = tokens.shape[1]
    tok_f32 = tokens.astype(jnp.float32)
    square_part = jnp.sum(tok_f32 * tok_f32, axis=-1)
    gain_part = lax.dynamic_slice_in_dim(norm_gain, lax.axis_index("tp") * quarter, quarter)
    tok_normed = (tok_f32 * gain_part).astype(jnp.bfloat16)
    query_part = jnp.dot(tok_normed, query_weight, preferred_element_type=jnp.float32)
    new_part = jnp.dot(tok_normed, key_value_weight, preferred_element_type=jnp.float32)
    query_sum, new_sum, square_sum = (
        lax.psum_scatter(
            query_part.reshape(steps, group_rows, -1), "tp", scatter_dimension=1, tiled=True
        ),
        lax.psum_scatter(
            new_part.reshape(steps, group_rows, -1), "tp", scatter_dimension=1, tiled=True
        ),
        lax.psum_scatter(
            square_part.reshape(steps, group_rows), "tp", scatter_dimension=1, tiled=True
        ),
    )
    tok_scale = lax.rsqrt(square_sum / MODEL_WIDTH + EPSILON)[..., None]
    request_list = query_sum.shape[1]
    heads_per_group = query_sum.shape[2] // HEAD_SIZE
    query_rows = (
        (tok_scale * query_sum)
        .astype(jnp.bfloat16)
        .reshape(steps, request_list, heads_per_group, HEAD_SIZE)
    )
    fresh_key_value = (tok_scale * new_sum).astype(jnp.bfloat16)
    new_keys = fresh_key_value[..., :HEAD_SIZE]
    new_values = fresh_key_value[..., HEAD_SIZE:]
    cache_keys = key_value_cache[..., :HEAD_SIZE]
    cache_values = key_value_cache[..., HEAD_SIZE:]
    inverse_root = 1.0 / math.sqrt(HEAD_SIZE)
    old_scores = (
        jnp.einsum("srqd,rcd->srqc", query_rows, cache_keys, preferred_element_type=jnp.float32)
        * inverse_root
    )
    new_scores = (
        jnp.einsum("srqd,trd->srqt", query_rows, new_keys, preferred_element_type=jnp.float32)
        * inverse_root
    )
    step_ids = lax.iota(jnp.int32, steps)
    allowed = (step_ids[None, :] <= step_ids[:, None])[:, None, None, :]
    new_masked = jnp.where(allowed, new_scores, -1e30)
    top = jnp.maximum(
        jnp.max(old_scores, axis=-1, keepdims=True), jnp.max(new_masked, axis=-1, keepdims=True)
    )
    old_weights = jnp.exp(old_scores - top)
    new_weights = jnp.where(allowed, jnp.exp(new_scores - top), 0.0)
    total = jnp.sum(old_weights, axis=-1, keepdims=True) + jnp.sum(
        new_weights, axis=-1, keepdims=True
    )
    old_probs = (old_weights / total).astype(jnp.bfloat16)
    new_probs = (new_weights / total).astype(jnp.bfloat16)
    mixed = jnp.einsum(
        "srqc,rcd->srqd", old_probs, cache_values, preferred_element_type=jnp.float32
    )
    mixed = mixed + jnp.einsum(
        "srqt,trd->srqd", new_probs, new_values, preferred_element_type=jnp.float32
    )
    attended = mixed.reshape(steps, request_list, heads_per_group * HEAD_SIZE).astype(jnp.bfloat16)
    return (attended, fresh_blocks)


def solution(mesh):
    in_specs = (
        P(("grp", "tp"), None),
        P(),
        P("tp", "pool"),
        P("tp", "pool"),
        P(("grp", "tp")),
        P(("grp", "tp"), None),
        P("pool", "tp"),
        P(None, "grp"),
        P(("grp", "tp"), None, "pool"),
    )
    out_specs = (P(None, ("grp", "tp"), "pool"), P("grp", "tp", None, None, None, "pool"))
    return jax.shard_map(shards, mesh=mesh, in_specs=in_specs, out_specs=out_specs, check_vma=False)
```

profile of v0, /device:TPU:1, one launch (start us, length us, event | category | flops | bytes accessed | tf_op | source)
XLA Modules:
  0.0 258.8 jit_solution(10241391948755742261)
XLA Ops:
  8.1 2.5 convolution_convert_fusion.1
  10.7 0.5 all-gather.2.cloned.1.call-update
  11.3 97.0 %all-reduce.4.cloned.1.call-done = bf16[512,896]{1,0:T(8,128)(2,1)} async-done(((bf16[512,896]{1,0:T(8,128)(2,1)}), bf16[512,896]{1,0:T(8,128)(2,1)}) %all-reduce.4.cloned.1.call-update) | async-done | bytes 917520 | tf_op jit(solution)/shard_map/psum | solution.py:74
  108.3 1.4 fusion.2
  109.8 0.7 copy.33
  110.6 1.7 fusion.17
  112.3 1.1 copy.24
  113.5 2.4 fusion.19
  116.0 0.6 copy-done.6
  116.8 1.3 dynamic-slice
  119.5 2.8 %fusion.14 = bf16[256,256]{1,0:T(8,128)(2,1)} fusion(bf16[3584,256]{1,0:T(8,128)(2,1)} %all-gather.2.cloned.1.call-done, bf16[256,3584]{1,0:T(8,128)(2,1)S(1)} %copy-done.1, f32[3584]{0:T(1024)S(1)} %copy-done.5, f32[256]{0:T(256)S(1)} %add_rsqrt_fusion.1), kind=kOutput, calls=%fused_computation.21 | convolution fusion | flops 472645632 | bytes 3816448 | tf_op jit(solution)/shard_map/dot_general | solution.py:29
  122.3 1.0 reshape.139
  123.6 0.7 copy.27
  124.3 9.2 %all-to-all-start = ((bf16[32,2,8,256]{3,2,1,0:T(8,128)(2,1)}), bf16[32,2,8,256]{3,2,1,0:T(8,128)(2,1)S(1)}, u32[]{:S(2)}, u32[]{:S(2)}) async-start(bf16[32,2,8,256]{3,2,1,0:T(8,128)(2,1)} %copy.27), calls=%async_computation.1 | async-start | bytes 524288 | tf_op jit(solution)/shard_map/all_to_all | solution.py:65
  133.5 0.5 reduce-scatter.7.cloned.1.call-done
  133.9 0.8 copy.34
  134.8 58.6 %all-reduce.6.cloned.1.call-done = f32[4,128,256]{2,0,1:T(4,128)} async-done(((f32[4,128,256]{2,0,1:T(4,128)}), f32[4,128,256]{2,0,1:T(4,128)}) %all-reduce.6.cloned.1.call-update) | async-done | bytes 524304
  193.5 1.0 fusion.30
  194.5 50.2 %reduce-scatter.5.cloned.1.call-done = f32[4,32,896]{2,1,0:T(8,128)} async-done(((f32[4,128,896]{2,1,0:T(8,128)}), f32[4,32,896]{2,1,0:T(8,128)}) %reduce-scatter.5.cloned.1.call-update) | async-done | bytes 458768 | tf_op jit(solution)/shard_map/reduce_scatter | solution.py:83
  244.6 1.1 multiply_convert_fusion
  246.4 1.3 select_reduce_fusion
  248.5 0.7 convolution_bitcast_fusion.1
  249.8 0.7 copy.32
  250.5 0.7 copy.48
  (49 shorter events, 3.6 us)
Async XLA Ops:
  8.0 105.5 %copy-start = (bf16[896,896]{1,0:T(8,128)(2,1)S(1)}, bf16[896,896]{1,0:T(8,128)(2,1)}, u32[]{:S(2)}) copy-start(bf16[896,896]{1,0:T(8,128)(2,1)} %param.12) | copy-start | bytes 4816900
  8.0 102.6 %copy-start.3 = (bf16[896,256]{1,0:T(8,128)(2,1)S(1)}, bf16[896,256]{1,0:T(8,128)(2,1)}, u32[]{:S(2)}) copy-start(bf16[896,256]{1,0:T(8,128)(2,1)} %param.11) | copy-start | bytes 1376260
  8.0 3.2 %copy-start.5 = (f32[3584]{0:T(1024)S(1)}, f32[3584]{0:T(1024)}, u32[]{:S(2)}) copy-start(f32[3584]{0:T(1024)} %param.10) | copy-start | bytes 43012
  8.0 100.3 %all-reduce.4.cloned.1.call-start = ((), (), s32[]{:S(2)}) async-start(), calls=%async_computation.3 | async-start | bytes 1835008 | tf_op jit(solution)/shard_map/psum | solution.py:74
  10.6 108.9 %all-gather.2.cloned.1.call-start = ((), (), s32[]{:S(2)}) async-start(), calls=%async_computation.5 | async-start | bytes 2293760 | tf_op jit(solution)/shard_map/all_gather | solution.py:31
  11.2 122.8 %reduce-scatter.7.cloned.1.call-start = ((), (), s32[]{:S(2)}) async-start(), calls=%async_computation.6 | async-start | bytes 81920
  110.5 3.0 %copy-start.2 = (bf16[512,896]{1,0:T(8,128)(2,1)S(1)}, bf16[512,896]{1,0:T(8,128)(2,1)}, u32[]{:S(2)}) copy-start(bf16[512,896]{1,0:T(8,128)(2,1)} %all-reduce.4.cloned.1.call-done) | copy-start | bytes 2752516
  110.5 82.9 %all-reduce.6.cloned.1.call-start = ((), (), s32[]{:S(2)}) async-start(), calls=%async_computation.7 | async-start | bytes 1048576
  113.4 131.2 %reduce-scatter.5.cloned.1.call-start = ((), (), s32[]{:S(2)}) async-start(), calls=%async_computation.4 | async-start | bytes 2293760 | tf_op jit(solution)/shard_map/reduce_scatter | solution.py:83
  115.9 0.7 copy-start.6
  115.9 2.8 %copy-start.7 = (s32[32,1]{0,1:T(1,128)S(1)}, s32[32,1]{0,1:T(1,128)}, u32[]{:S(2)}) copy-start(s32[32,1]{0,1:T(1,128)} %param.14) | copy-start | bytes 388
  115.9 3.0 %copy-start.1 = (bf16[256,3584]{1,0:T(8,128)(2,1)S(1)}, bf16[256,3584]{1,0:T(8,128)(2,1)}, u32[]{:S(2)}) copy-start(bf16[256,3584]{1,0:T(8,128)(2,1)} %param.9) | copy-start | bytes 5505028
  122.3 123.8 %copy-start.4 = (bf16[32,16,256]{2,1,0:T(8,128)(2,1)S(1)}, bf16[32,16,256]{2,1,0:T(8,128)(2,1)}, u32[]{:S(2)}) copy-start(bf16[32,16,256]{2,1,0:T(8,128)(2,1)} %param.17) | copy-start | bytes 786436
  124.3 70.2 %all-to-all-start = ((bf16[32,2,8,256]{3,2,1,0:T(8,128)(2,1)}), bf16[32,2,8,256]{3,2,1,0:T(8,128)(2,1)S(1)}, u32[]{:S(2)}, u32[]{:S(2)}) async-start(bf16[32,2,8,256]{3,2,1,0:T(8,128)(2,1)} %copy.27), calls=%async_computation.1 | async-start | bytes 524288 | tf_op jit(solution)/shard_map/all_to_all | solution.py:65
Sparse Core Ops, SparseCore 0:
  11.8 96.4 all-reduce.3
Sparse Core Ops, SparseCore 1:
  13.2 66.1 all-gather.1
  110.6 23.3 reduce-scatter.6
  137.0 56.4 all-reduce.5
  196.6 48.0 reduce-scatter.4
where the time goes:
time: 259 us
  waiting for transfers between devices  207 us (80%)
  between operations  16.6 us (6%)
  matrix products  12.4 us (5%)
  starting transfers between devices  9.39 us (4%)
  local copies, waits for them, and re-layouts  8.48 us (3%)
  other arithmetic  5.05 us (2%)
    psum x1, waiting for transfers between devices, shards(): tokens = lax.psum(partial_rows.astype(jnp.bfloat16), 'pool')  97 us
    unnamed x7, waiting for transfers between devices  59.7 us
    reduce_scatter x1, waiting for transfers between devices, shards(): lax.psum_scatter(query_part.reshape(steps, group_rows, -1), 'tp', scatter...  50.2 us
    all_to_all x1, starting transfers between devices, shards(): lax.all_to_all(outgoing, 'grp', split_axis=0, concat_axis=0, tiled=True)  9.18 us
  transfers between devices with their start and end apart: 6, of which 4 were waited for; matrix products, arithmetic and copies ran while one was open for 6% of the time, Pallas kernels for 0%

commit v1 on v0

v1 whole, which is shorter than its diff:
```python
import math

import jax
import jax.numpy as jnp
from jax import lax
from jax.sharding import Mesh, PartitionSpec as P

MODEL_WIDTH = 3584
HEAD_SIZE = 128
EPSILON = 1e-06
BF16 = jnp.bfloat16
F32 = jnp.float32


def spread(x, axes, number):
    copies = jnp.broadcast_to(x[None], (number,) + x.shape)
    return lax.all_to_all(copies, axes, 0, 0, tiled=True)


def code_projection(table, gain_part, query_weight, key_value_weight):
    z, x = lax.axis_index("z"), lax.axis_index("x")
    groups = lax.axis_size("z") * lax.axis_size("x")
    cores, halves = lax.axis_size("core"), lax.axis_size("yh")
    local_codes = table.shape[0]
    share = local_codes // groups
    group = z * lax.axis_size("x") + x
    mine = lax.dynamic_slice_in_dim(table, group * share, share)
    rows = spread(mine, ("yh", "core"), halves * cores).reshape(halves * cores * share, -1)
    rows_f32 = rows.astype(F32)
    square = jnp.sum(rows_f32 * rows_f32, axis=-1, keepdims=True)
    normed = (rows_f32 * gain_part).astype(BF16)
    part = jnp.concatenate(
        [
            jnp.dot(normed, query_weight, preferred_element_type=F32),
            jnp.dot(normed, key_value_weight, preferred_element_type=F32),
            jnp.broadcast_to(square, (square.shape[0], HEAD_SIZE)),
        ],
        axis=1,
    )
    total = jnp.sum(spread(part, "tp", lax.axis_size("tp")), axis=0)
    scale = lax.rsqrt(total[:, -1:] / MODEL_WIDTH + EPSILON)
    projected = (scale * total[:, :-HEAD_SIZE]).astype(BF16)
    plane = spread(projected, "z", lax.axis_size("z"))
    whole = spread(plane, "x", lax.axis_size("x"))
    xs, zs, ps, js = (
        lax.broadcasted_iota(jnp.int32, (lax.axis_size("x"), lax.axis_size("z"), halves * cores, share), d)
        for d in range(4)
    )
    codes = ps * local_codes + (zs * lax.axis_size("x") + xs) * share + js
    return whole.reshape(codes.size, -1), codes.reshape(-1)


def shards(
    history,
    norm_gain,
    key_value_weight,
    query_weight,
    live_count,
    owner_group,
    code_table,
    code_ids,
    key_value_cache,
):
    key_value_width = key_value_weight.shape[1]
    quarter = code_table.shape[1]
    gain_part = lax.dynamic_slice_in_dim(norm_gain, lax.axis_index("tp") * quarter, quarter)
    whole_weight = spread(key_value_weight, "tp", lax.axis_size("tp")).reshape(-1, key_value_width)

    projected, codes = code_projection(code_table, gain_part, query_weight, key_value_weight)

    hist_f32 = history.astype(F32)
    hist_scale = lax.rsqrt(jnp.mean(hist_f32 * hist_f32, axis=-1, keepdims=True) + EPSILON)
    hist_normed = (hist_f32 * norm_gain).astype(BF16)
    kv_sum = jnp.dot(hist_normed, whole_weight, preferred_element_type=F32)
    hist_kv = (hist_scale * kv_sum).astype(BF16)
    blocks_here = live_count.shape[0]
    block_len = history.shape[0] // blocks_here
    groups = lax.axis_size("z") * lax.axis_size("x")
    capacity = max(2, 2 * blocks_here // groups)
    events = lax.broadcasted_iota(jnp.int32, (blocks_here, block_len), 1)
    keep = events < live_count[:, None]
    blocks = jnp.where(
        keep[:, :, None],
        hist_kv.reshape(blocks_here, block_len, key_value_width),
        jnp.zeros((), BF16),
    )
    target = owner_group[:, 0]
    same_target = target[:, None] == target[None, :]
    order = lax.iota(jnp.int32, blocks_here)
    earlier = order[None, :] < order[:, None]
    rank = jnp.sum((same_target & earlier).astype(jnp.int32), axis=1)
    group_ids = lax.iota(jnp.int32, groups)
    slot_ids = lax.iota(jnp.int32, capacity)
    select = (
        (target[None, None, :] == group_ids[:, None, None])
        & (rank[None, None, :] == slot_ids[None, :, None])
    ).astype(BF16)
    outgoing = jnp.einsum(
        "gkb,bx->gkx",
        select,
        blocks.reshape(blocks_here, block_len * key_value_width),
        preferred_element_type=F32,
    )
    outgoing = outgoing.astype(BF16).reshape(groups, capacity, block_len, key_value_width)
    received = lax.all_to_all(outgoing, ("z", "x"), 0, 0, tiled=True)
    fresh_blocks = received[None, None]

    steps = code_ids.shape[0]
    request_list = code_ids.shape[1] // lax.axis_size("tp")
    ids = lax.dynamic_slice_in_dim(code_ids, lax.axis_index("tp") * request_list, request_list, 1)
    one_hot = (ids.reshape(-1)[:, None] == codes[None, :]).astype(BF16)
    tokens = jnp.dot(one_hot, projected, preferred_element_type=F32).astype(BF16)
    heads_per_group = (tokens.shape[1] - key_value_width) // HEAD_SIZE
    query_rows = tokens[:, :-key_value_width].reshape(steps, request_list, heads_per_group, HEAD_SIZE)
    fresh_key_value = tokens[:, -key_value_width:].reshape(steps, request_list, key_value_width)
    new_keys = fresh_key_value[..., :HEAD_SIZE]
    new_values = fresh_key_value[..., HEAD_SIZE:]
    cache_keys = key_value_cache[..., :HEAD_SIZE]
    cache_values = key_value_cache[..., HEAD_SIZE:]
    inverse_root = 1.0 / math.sqrt(HEAD_SIZE)
    old_scores = (
        jnp.einsum("srqd,rcd->srqc", query_rows, cache_keys, preferred_element_type=F32)
        * inverse_root
    )
    new_scores = (
        jnp.einsum("srqd,trd->srqt", query_rows, new_keys, preferred_element_type=F32)
        * inverse_root
    )
    step_ids = lax.iota(jnp.int32, steps)
    allowed = (step_ids[None, :] <= step_ids[:, None])[:, None, None, :]
    new_masked = jnp.where(allowed, new_scores, -1e30)
    top = jnp.maximum(
        jnp.max(old_scores, axis=-1, keepdims=True), jnp.max(new_masked, axis=-1, keepdims=True)
    )
    old_weights = jnp.exp(old_scores - top)
    new_weights = jnp.where(allowed, jnp.exp(new_scores - top), 0.0)
    total = jnp.sum(old_weights, axis=-1, keepdims=True) + jnp.sum(
        new_weights, axis=-1, keepdims=True
    )
    old_probs = (old_weights / total).astype(BF16)
    new_probs = (new_weights / total).astype(BF16)
    mixed = jnp.einsum("srqc,rcd->srqd", old_probs, cache_values, preferred_element_type=F32)
    mixed = mixed + jnp.einsum("srqt,trd->srqd", new_probs, new_values, preferred_element_type=F32)
    attended = mixed.reshape(steps, request_list, heads_per_group * HEAD_SIZE).astype(BF16)
    return (attended, fresh_blocks)


def solution(mesh):
    halves, cores = 2, 2
    depth, across = 8, 4
    split = Mesh(
        mesh.devices.reshape(halves, cores, depth, across, mesh.shape["tp"]),
        ("yh", "core", "z", "x", "tp"),
    )
    pool, grp = ("yh", "core"), ("z", "x")
    rows = grp + ("tp",)
    in_specs = (
        P(rows, None),
        P(),
        P("tp", pool),
        P("tp", pool),
        P(rows),
        P(rows, None),
        P(pool, "tp"),
        P(None, grp),
        P(rows, None, pool),
    )
    out_specs = (P(None, rows, pool), P(grp, "tp", None, None, None, pool))
    return jax.shard_map(shards, mesh=split, in_specs=in_specs, out_specs=out_specs, check_vma=False)
```

time: 259 us -> 139 us (0.54)
  waiting for transfers between devices: 207 us -> 63 us
  blocking collectives: 0 us -> 29.5 us
  starting transfers between devices: 9.39 us -> 26.2 us
  between operations: 16.6 us -> 0.9 us
  matrix products: 12.4 us -> 6.58 us
    psum x1 -> x0, waiting for transfers between devices: 97 us -> none  [shards(): tokens = lax.psum(partial_rows.astype(jnp.bfloat16), 'pool')]
    all_to_all x1 -> x4, waiting for transfers between devices: 0.01 us -> 63 us  [the longest x3 54.6 us: spread(): return lax.all_to_all(copies, axes, 0, 0, tiled=True)]
    unnamed x7 -> x0, waiting for transfers between devices: 59.7 us -> none
    reduce_scatter x1 -> x0, waiting for transfers between devices: 50.2 us -> none  [shards(): lax.psum_scatter(query_part.reshape(steps, group_rows, -1), 'tp', scatter...]
    all_to_all x0 -> x2, blocking collectives: none -> 29.5 us  [spread(): return lax.all_to_all(copies, axes, 0, 0, tiled=True)]
    all_to_all x1 -> x4, starting transfers between devices: 9.18 us -> 26.2 us  [the longest x3 19.6 us: spread(): return lax.all_to_all(copies, axes, 0, 0, tiled=True)]
    dot_general x4, matrix products: 9.41 us -> 3.57 us  [the longest x1 2.69 us: shards(): kv_sum = jnp.dot(hist_normed, whole_weight, preferred_element_type=F32)]
    unnamed x22 -> x17, local copies, waits for them, and re-layouts: 4.23 us -> 0.82 us
  transfers between devices with their start and end apart: 6 -> 4, of which waited for: 4 -> 4; matrix products, arithmetic and copies ran while one was open for 6% -> 6% of each run, Pallas kernels for 0% -> 0%
where the time goes in v1:
time: 139 us; the launch traced here: 138 us
  waiting for transfers between devices  63 us (45%)
  blocking collectives  29.5 us (21%)
  starting transfers between devices  26.2 us (19%)
  local copies, waits for them, and re-layouts  8.05 us (6%)
  matrix products  6.58 us (5%)
  other arithmetic  3.51 us (3%)
    all_to_all x3, waiting for transfers between devices, spread(): return lax.all_to_all(copies, axes, 0, 0, tiled=True)  54.6 us
    all_to_all x2, blocking collectives, spread(): return lax.all_to_all(copies, axes, 0, 0, tiled=True)  29.5 us
    all_to_all x3, starting transfers between devices, spread(): return lax.all_to_all(copies, axes, 0, 0, tiled=True)  19.6 us
    all_to_all x1, waiting for transfers between devices, shards(): received = lax.all_to_all(outgoing, ('z', 'x'), 0, 0, tiled=True)  8.43 us
    all_to_all x1, starting transfers between devices, shards(): received = lax.all_to_all(outgoing, ('z', 'x'), 0, 0, tiled=True)  6.61 us
    broadcast_in_dim x5, local copies, waits for them, and re-layouts, spread(): copies = jnp.broadcast_to(x[None], (number,) + x.shape)  3.11 us
  transfers between devices with their start and end apart: 4, of which 4 were waited for; matrix products, arithmetic and copies ran while one was open for 6% of the time, Pallas kernels for 0%

profile of v1, /device:TPU:1, one launch (start us, length us, event | category | flops | bytes accessed | tf_op | source)
XLA Modules:
  0.0 137.8 jit_solution(15859170712028947342)
XLA Ops:
  0.7 0.9 constant_dynamic-slice_fusion
  1.5 0.6 broadcast_in_dim.46
  2.2 10.1 %all-to-all-start = ((bf16[4,4,896]{2,1,0:T(4,128)(2,1)}), bf16[4,4,896]{2,1,0:T(4,128)(2,1)S(1)}, u32[]{:S(2)}, u32[]{:S(2)}) async-start(bf16[4,4,896]{2,1,0:T(4,128)(2,1)} %broadcast_in_dim.46), calls=%async_computation | async-start | bytes 57344 | tf_op jit(solution)/shard_map/all_to_all | solution.py:17
  12.3 0.8 dynamic_slice.11
  13.0 6.3 %all-to-all-done = bf16[4,4,896]{2,1,0:T(4,128)(2,1)S(1)} async-done(((bf16[4,4,896]{2,1,0:T(4,128)(2,1)}), bf16[4,4,896]{2,1,0:T(4,128)(2,1)S(1)}, u32[]{:S(2)}, u32[]{:S(2)}) %all-to-all-start) | async-done | bytes 28704 | tf_op jit(solution)/shard_map/all_to_all | solution.py:17
  20.2 11.4 %all_to_all.30 = f32[4,16,1280]{2,1,0:T(8,128)S(1)} all-to-all(f32[4,16,1280]{2,1,0:T(8,128)S(1)} %broadcast_in_dim.49), channel_id=1, replica_groups=mesh['yh'=2,'core'=2,'z'=8,'x'=4,'tp'=4] {'tp'}, dimensions={0} | all-to-all | bytes 655360 | tf_op jit(solution)/shard_map/all_to_all | solution.py:17
  31.9 18.1 %all_to_all.31 = bf16[8,16,1152]{2,1,0:T(8,128)(2,1)S(1)} all-to-all(bf16[8,16,1152]{2,1,0:T(8,128)(2,1)S(1)} %broadcast_in_dim.54), channel_id=1, replica_groups=mesh['yh'=2,'core'=2,'z'=8,'x'=4,'tp'=4] {'z'}, dimensions={0} | all-to-all | bytes 589824 | tf_op jit(solution)/shard_map/all_to_all | solution.py:17
  50.0 1.1 broadcast_in_dim.55
  51.1 4.0 %all-to-all-start.3 = ((bf16[4,8,16,1152]{3,2,1,0:T(8,128)(2,1)}), bf16[4,8,16,1152]{3,2,1,0:T(8,128)(2,1)S(1)}, u32[]{:S(2)}, u32[]{:S(2)}) async-start(bf16[4,8,16,1152]{3,2,1,0:T(8,128)(2,1)} %broadcast_in_dim.55), calls=%async_computation.3 | async-start | bytes 2359296 | tf_op jit(solution)/shard_map/all_to_all | solution.py:17
  55.3 12.0 %all-to-all-done.3 = bf16[4,8,16,1152]{3,2,1,0:T(8,128)(2,1)S(1)} async-done(((bf16[4,8,16,1152]{3,2,1,0:T(8,128)(2,1)}), bf16[4,8,16,1152]{3,2,1,0:T(8,128)(2,1)S(1)}, u32[]{:S(2)}, u32[]{:S(2)}) %all-to-all-start.3) | async-done | bytes 1179680 | tf_op jit(solution)/shard_map/all_to_all | solution.py:17
  67.3 1.3 broadcast_in_dim.103
  68.6 5.5 %all-to-all-start.4 = ((bf16[4,896,256]{2,1,0:T(8,128)(2,1)}), bf16[4,896,256]{2,1,0:T(8,128)(2,1)}, u32[]{:S(2)}, u32[]{:S(2)}) async-start(bf16[4,896,256]{2,1,0:T(8,128)(2,1)} %broadcast_in_dim.103), calls=%async_computation.4 | async-start | bytes 3670016 | tf_op jit(solution)/shard_map/all_to_all | solution.py:17
  74.8 1.9 %fusion = f32[256]{0:T(256)S(1)} fusion(bf16[256,3584]{1,0:T(8,128)(2,1)} %param.9), kind=kLoop, calls=%fused_computation.2 | loop fusion | flops 2752256 | bytes 1836032 | tf_op jit(solution)/shard_map/reduce_sum | solution.py:72
  77.5 1.3 select_reduce_fusion
  78.8 0.4 fusion.48
  79.5 0.4 fusion.15
  80.0 36.3 %all-to-all-done.4 = bf16[4,896,256]{2,1,0:T(8,128)(2,1)} async-done(((bf16[4,896,256]{2,1,0:T(8,128)(2,1)}), bf16[4,896,256]{2,1,0:T(8,128)(2,1)}, u32[]{:S(2)}, u32[]{:S(2)}) %all-to-all-start.4) | async-done | bytes 1835040 | tf_op jit(solution)/shard_map/all_to_all | solution.py:17
  116.3 2.7 %fusion.12 = bf16[256,256]{1,0:T(8,128)(2,1)S(1)} fusion(bf16[3584,256]{1,0:T(8,128)(2,1)} %bitcast.15, bf16[256,3584]{1,0:T(8,128)(2,1)} %param.9, f32[3584]{0:T(1024)S(1)} %copy-done.4, f32[256]{0:T(256)S(1)} %add_rsqrt_fusion), kind=kOutput, calls=%fused_computation.17 | convolution fusion | flops 472645632 | bytes 3816448 | tf_op jit(solution)/shard_map/dot_general | solution.py:74
  119.3 0.7 copy.36
  120.1 6.6 %all-to-all-start.5 = ((bf16[32,2,8,256]{3,2,1,0:T(8,128)(2,1)}), bf16[32,2,8,256]{3,2,1,0:T(8,128)(2,1)S(1)}, u32[]{:S(2)}, u32[]{:S(2)}) async-start(bf16[32,2,8,256]{3,2,1,0:T(8,128)(2,1)} %copy.36), calls=%async_computation.5 | async-start | bytes 524288 | tf_op jit(solution)/shard_map/all_to_all | solution.py:105
  126.7 0.7 convolution_bitcast_fusion.1
  127.9 0.7 copy.41
  128.7 8.4 %all-to-all-done.5 = bf16[32,2,8,256]{3,2,1,0:T(8,128)(2,1)S(1)} async-done(((bf16[32,2,8,256]{3,2,1,0:T(8,128)(2,1)}), bf16[32,2,8,256]{3,2,1,0:T(8,128)(2,1)S(1)}, u32[]{:S(2)}, u32[]{:S(2)}) %all-to-all-start.5) | async-done | bytes 262176 | tf_op jit(solution)/shard_map/all_to_all | solution.py:105
  137.1 0.7 copy.61
  (53 shorter events, 3.8 us)
Async XLA Ops:
  0.6 18.7 %copy-start = (bf16[896,896]{1,0:T(8,128)(2,1)S(1)}, bf16[896,896]{1,0:T(8,128)(2,1)}, u32[]{:S(2)}) copy-start(bf16[896,896]{1,0:T(8,128)(2,1)} %param.12) | copy-start | bytes 4816900
  0.6 19.0 %copy-start.1 = (bf16[896,256]{1,0:T(8,128)(2,1)S(1)}, bf16[896,256]{1,0:T(8,128)(2,1)}, u32[]{:S(2)}) copy-start(bf16[896,256]{1,0:T(8,128)(2,1)} %param.11) | copy-start | bytes 1376260
  2.2 17.2 %all-to-all-start = ((bf16[4,4,896]{2,1,0:T(4,128)(2,1)}), bf16[4,4,896]{2,1,0:T(4,128)(2,1)S(1)}, u32[]{:S(2)}, u32[]{:S(2)}) async-start(bf16[4,4,896]{2,1,0:T(4,128)(2,1)} %broadcast_in_dim.46), calls=%async_computation | async-start | bytes 57344 | tf_op jit(solution)/shard_map/all_to_all | solution.py:17
  50.0 5.1 %copy-start.3 = (s32[4,128]{1,0:T(4,128)S(1)}, s32[4,128]{1,0:T(4,128)}, u32[]{:S(2)}) copy-start(s32[4,128]{1,0:T(4,128)} %param.16) | copy-start | bytes 6148
  51.1 16.2 %all-to-all-start.3 = ((bf16[4,8,16,1152]{3,2,1,0:T(8,128)(2,1)}), bf16[4,8,16,1152]{3,2,1,0:T(8,128)(2,1)S(1)}, u32[]{:S(2)}, u32[]{:S(2)}) async-start(bf16[4,8,16,1152]{3,2,1,0:T(8,128)(2,1)} %broadcast_in_dim.55), calls=%async_computation.3 | async-start | bytes 2359296 | tf_op jit(solution)/shard_map/all_to_all | solution.py:17
  68.6 5.7 %copy-start.5 = (s32[32]{0:T(128)S(1)}, s32[32]{0:T(128)}, u32[]{:S(2)}) copy-start(s32[32]{0:T(128)} %param.13) | copy-start | bytes 388
  68.6 6.0 %copy-start.6 = (s32[32,1]{0,1:T(1,128)S(1)}, s32[32,1]{0,1:T(1,128)}, u32[]{:S(2)}) copy-start(s32[32,1]{0,1:T(1,128)} %param.14) | copy-start | bytes 388
  68.6 47.7 %all-to-all-start.4 = ((bf16[4,896,256]{2,1,0:T(8,128)(2,1)}), bf16[4,896,256]{2,1,0:T(8,128)(2,1)}, u32[]{:S(2)}, u32[]{:S(2)}) async-start(bf16[4,896,256]{2,1,0:T(8,128)(2,1)} %broadcast_in_dim.103), calls=%async_computation.4 | async-start | bytes 3670016 | tf_op jit(solution)/shard_map/all_to_all | solution.py:17
  76.7 2.1 %copy-start.2 = (bf16[32,16,256]{2,1,0:T(8,128)(2,1)S(1)}, bf16[32,16,256]{2,1,0:T(8,128)(2,1)}, u32[]{:S(2)}) copy-start(bf16[32,16,256]{2,1,0:T(8,128)(2,1)} %param.17) | copy-start | bytes 786436
  77.2 39.1 %copy-start.4 = (f32[3584]{0:T(1024)S(1)}, f32[3584]{0:T(1024)}, u32[]{:S(2)}) copy-start(f32[3584]{0:T(1024)} %param.10) | copy-start | bytes 43012
  120.1 17.0 %all-to-all-start.5 = ((bf16[32,2,8,256]{3,2,1,0:T(8,128)(2,1)}), bf16[32,2,8,256]{3,2,1,0:T(8,128)(2,1)S(1)}, u32[]{:S(2)}, u32[]{:S(2)}) async-start(bf16[32,2,8,256]{3,2,1,0:T(8,128)(2,1)} %copy.36), calls=%async_computation.5 | async-start | bytes 524288 | tf_op jit(solution)/shard_map/all_to_all | solution.py:105
